TPU v7x, 32 devices: a whole 2x2x4 slice. The times are simulated.
32 devices in a mesh: scalar: 4 (over z), space: 8 (over y, x, core).
Axes of the slice: x: 2, y: 2, z: 4, core: 2. Of those that a mesh axis runs over, the one named last changes fastest.
Arguments:
- scalars: float32 [16, 2, 1024, 1024], P('scalar', None, 'space'), may hold values from -6 to 6
- velocity_x: float32 [2, 1024, 1024], P(None, 'space', 'scalar'), may hold values from 0 to 1, as said below
- velocity_y: float32 [2, 1024, 1024], P(None, 'space', 'scalar'), may hold values from 0 to 1, as said below
- shift_x: int32 [2, 1024], P(None, 'space'), may hold values from -8 to 8
- shift_y: int32 [1024], P('space'), may hold values from -8 to 8
- schmidt: int32 [16], P('scalar'), may hold values from 1 to 5
Outputs:
- transported: float32 [16, 2, 1024, 1024], P('scalar', None, 'space')
Inputs may be any that keep to these rules, and one draw needn't show every extreme that they name: shift_x and shift_y are whole cells of displacement along the line; they act periodically. `velocity_x`: fractions of a cell. `velocity_y`: fractions of a cell.
All inputs are finite; a program needn't handle non-finite values.
Results may differ from a plain program's by a relative error of at most 0.0003.
Values sent between devices are 32-bit elements; how exact they have to be, the bound alone decides.
A program may use at most 192 MiB of HBM per device.

v0:
```python
import functools
import math

import jax
import jax.numpy as jnp
import numpy as np
from jax import lax
from jax.experimental import pallas as pl
from jax.experimental.pallas import tpu as pltpu
from jax.sharding import PartitionSpec as P

NY = 1024


def spline(distance):
    magnitude = jnp.abs(distance)
    far_part = jnp.maximum(3.0 - magnitude, 0.0)
    middle = jnp.maximum(2.0 - magnitude, 0.0)
    near_part = jnp.maximum(1.0 - magnitude, 0.0)
    return (far_part**5 - 6.0 * middle**5 + 15.0 * near_part**5) / 120.0


def remesh(fields, fraction, shift_line):
    summed = jnp.zeros_like(fields)
    for offset in range(-2, 4):
        weight = spline(offset - fraction)
        summed = summed + jnp.roll(fields * weight, offset, axis=-1)
    line_shift = shift_line[None, :, :, None]
    moved = summed
    for amount in range(-8, 9):
        moved = jnp.where(line_shift == amount, jnp.roll(summed, amount, axis=-1), moved)
    return moved


def remesh_columns(fields, fraction, shift_cols):
    summed = jnp.zeros_like(fields)
    for offset in range(-2, 4):
        weight = spline(offset - fraction)
        summed = summed + jnp.roll(fields * weight[None], offset, axis=2)
    column_shift = shift_cols[None, None, None, :]
    moved = summed
    for amount in range(-8, 9):
        moved = jnp.where(column_shift == amount, jnp.roll(summed, amount, axis=2), moved)
    return moved


def spectral_tables(length):
    midpoint = length // 2
    column = jnp.arange(length, dtype=jnp.int32)
    wavenum = jnp.where(column <= midpoint, column, column - midpoint)
    phases = column[:, None] * wavenum[None, :] % length
    angles = phases.astype(jnp.float32) * (2.0 * math.pi / length)
    forward = jnp.where((column <= midpoint)[None, :], jnp.cos(angles), jnp.sin(angles))
    inverse_weight = jnp.where((wavenum == 0) | (column == midpoint), 1.0, 2.0) / length
    inverse = forward.T * inverse_weight[:, None]
    relative = wavenum.astype(jnp.float32) / midpoint
    return (forward, inverse, relative * relative)


def diffuse(fields, diffusivity, tables):
    forward, inverse, wave_square = tables
    initial = fields.shape
    rows_flat = fields.reshape(-1, initial[-1])
    spectra = jnp.dot(
        rows_flat, forward, precision=lax.Precision.HIGHEST, preferred_element_type=jnp.float32
    )
    damping = jnp.exp(-diffusivity[:, None] * wave_square[None, :])
    spectra = spectra.reshape(initial) * damping[:, None, None, :]
    result = jnp.dot(
        spectra.reshape(-1, initial[-1]),
        inverse,
        precision=lax.Precision.HIGHEST,
        preferred_element_type=jnp.float32,
    )
    return result.reshape(initial)


def diffuse_columns(fields, diffusivity, tables):
    forward, inverse, wave_square = tables
    spectra = jnp.einsum(
        "jk,szjx->szkx",
        forward,
        fields,
        precision=lax.Precision.HIGHEST,
        preferred_element_type=jnp.float32,
    )
    damping = jnp.exp(-diffusivity[:, None] * wave_square[None, :])
    spectra = spectra * damping[:, None, :, None]
    return jnp.einsum(
        "kj,szkx->szjx",
        inverse,
        spectra,
        precision=lax.Precision.HIGHEST,
        preferred_element_type=jnp.float32,
    )


def one_sweep(fields, fraction, shift_line, diffusivity, tables):
    return diffuse(remesh(fields, fraction, shift_line), diffusivity, tables)


def fetch_velocity(velocity_x):
    return lax.all_gather(velocity_x, "scalar", axis=2, tiled=True)


def on_device(scalars, velocity_x, velocity_y, shift_x, shift_y, schmidt):
    diffusivity = jnp.exp2((3 - schmidt).astype(jnp.float32))
    tables_x = spectral_tables(scalars.shape[3])
    tables_y = spectral_tables(NY)
    along_x = fetch_velocity(velocity_x)
    fields = one_sweep(scalars, along_x, shift_x, 0.5 * diffusivity, tables_x)
    along_y = lax.all_gather(velocity_y, "scalar", axis=2, tiled=True)
    fields_cols, velocity_cols = (
        lax.all_to_all(fields, "space", split_axis=3, concat_axis=2, tiled=True),
        lax.all_to_all(along_y[None], "space", split_axis=3, concat_axis=2, tiled=True),
    )
    remeshed = remesh_columns(fields_cols, velocity_cols[0], shift_y)
    returned = diffuse_columns(remeshed, diffusivity, tables_y)
    fields = lax.all_to_all(returned, "space", split_axis=2, concat_axis=3, tiled=True)
    along_x = fetch_velocity(velocity_x)
    return one_sweep(fields, along_x, shift_x, 0.5 * diffusivity, tables_x)


BLOCK = 256
REACH = 8
MESH = pl.DeviceIdType.MESH


def spline_weights(f):
    g = 1.0 - f

    def fifth(v):
        w = v * v
        return w * w * v

    f0, f1, f2 = fifth(f), fifth(1.0 + f), fifth(2.0 + f)
    g0, g1, g2 = fifth(g), fifth(1.0 + g), fifth(2.0 + g)
    c = 1.0 / 120.0
    return (
        g0 * c,
        (g1 - 6.0 * g0) * c,
        (g2 - 6.0 * g1 + 15.0 * g0) * c,
        (f2 - 6.0 * f1 + 15.0 * f0) * c,
        (f1 - 6.0 * f0) * c,
        f0 * c,
    )


def response(kappa, length):
    half = length // 2
    k = np.arange(half + 1)
    weight = np.where((k == 0) | (k == half), 1.0, 2.0) / length
    phase = (k[:, None] * np.arange(length)[None, :]) % length
    table = (np.cos(phase * (2.0 * np.pi / length)) * weight[:, None]).astype(np.float32)
    relative = jnp.arange(half + 1).astype(jnp.float32) / half
    damping = jnp.exp(-kappa[:, None] * relative * relative)
    return jnp.dot(damping, table, precision=lax.Precision.HIGHEST, preferred_element_type=jnp.float32)


def circulant_kernel(g_ref, hi_ref, lo_ref):
    length = g_ref.shape[-1]
    wide = jnp.broadcast_to(g_ref[0], (BLOCK, length))
    turned = pltpu.roll(wide, 0, 1, stride=1, stride_axis=0)
    high = turned.astype(jnp.bfloat16)
    hi_ref[0] = high
    lo_ref[0] = (turned - high.astype(jnp.float32)).astype(jnp.bfloat16)


def circulant_blocks(g):
    count, length = g.shape
    spec = pl.BlockSpec((1, BLOCK, length), lambda i: (i, 0, 0))
    return pl.pallas_call(
        circulant_kernel,
        grid=(count,),
        in_specs=[pl.BlockSpec((1, 1, length), lambda i: (i, 0, 0))],
        out_specs=[spec, spec],
        out_shape=[jax.ShapeDtypeStruct((count, BLOCK, length), jnp.bfloat16)] * 2,
    )(g[:, None, :])


def halves(v):
    high = v.astype(jnp.bfloat16)
    return high, (v - high.astype(jnp.float32)).astype(jnp.bfloat16)


def dot32(a, b):
    return jnp.dot(a, b, preferred_element_type=jnp.float32)


def sweeps_kernel(
    peers, groups,
    q_ref, vx_ref, vy_ref, sx_ref, sy_ref, xh_ref, xl_ref, yh_ref, yl_ref,
    out_ref,
    wx, wy, part_hi, part_lo, swept, col_hi, col_lo, tall,
    ext, cols, turned, back, held,
    sendv, recvv, send1, recv1, send2, recv2,
):
    ns, nz, rows, nx = q_ref.shape
    ny = rows * peers
    width = nx // peers
    me = lax.axis_index("space")
    bx, by = nx // BLOCK, ny // BLOCK

    barrier = pltpu.get_barrier_semaphore()
    for k in range(1, peers):
        pl.semaphore_signal(barrier, inc=1, device_id={"space": lax.rem(me + k, peers)}, device_id_type=MESH)
    mine = lax.axis_index("scalar")
    for k in range(1, groups):
        pl.semaphore_signal(barrier, inc=1, device_id={"scalar": lax.rem(mine + k, groups)}, device_id_type=MESH)
    pl.semaphore_wait(barrier, peers + groups - 2)

    def spread(n, k):
        return pltpu.make_async_remote_copy(
            src_ref=(vx_ref, vy_ref)[n], dst_ref=held.at[n, mine],
            send_sem=sendv.at[n, k - 1], recv_sem=recvv.at[n, k - 1],
            device_id={"scalar": lax.rem(mine + k, groups)}, device_id_type=MESH,
        )

    for n in range(2):
        for k in range(1, groups):
            spread(n, k).start()
    held[0, mine] = vx_ref[...]
    held[1, mine] = vy_ref[...]

    step = 16
    per = rows // step

    def weigh(n, w_ref):
        for k in range(1, groups):
            spread(n, k).wait_recv()

        @pl.loop(0, nz * per)
        def _(i):
            z, r = i // per, pl.multiple_of((i % per) * step, step)
            f = jnp.concatenate([held[n, g, z, pl.ds(r, step), :] for g in range(groups)], axis=1)
            for m, w in enumerate(spline_weights(f)):
                w_ref[z, m, pl.ds(r, step), :] = w

    weigh(0, wx)

    def remesh_rows(load):
        @pl.loop(0, nz * per, unroll=2)
        def _(i):
            z, r = i // per, pl.multiple_of((i % per) * step, step)
            q = load(z, r)
            acc = q * wx[z, 0, pl.ds(r, step), :]
            for m in range(1, 6):
                acc = acc + pltpu.roll(q * wx[z, m, pl.ds(r, step), :], m, 1)
            shift = sx_ref[z, pl.ds(r, step), :] + REACH
            for places, low in (((1, 2, 3), 3), ((4, 8, 12, 16), 28)):
                now, base = shift & low, acc
                for place in places:
                    acc = jnp.where(now == place, pltpu.roll(base, place, 1), acc)
            at = pl.multiple_of(z * rows + r, step)
            part_hi[pl.ds(at, step), :], part_lo[pl.ds(at, step), :] = halves(acc)

    def diffuse_rows(s, store):
        for b in range(bx):
            total = jnp.zeros((nz * rows, BLOCK), jnp.float32)
            for a in range(bx):
                d = ((b - a) % bx) * BLOCK
                high, low = xh_ref[s, :, d:d + BLOCK], xl_ref[s, :, d:d + BLOCK]
                left = part_hi[:, a * BLOCK:(a + 1) * BLOCK]
                rest = part_lo[:, a * BLOCK:(a + 1) * BLOCK]
                total = total + (dot32(left, high) + (dot32(left, low) + dot32(rest, high)))
            store(b * BLOCK, total)

    def forward(s, k):
        dest = lax.rem(me + k, peers)
        return pltpu.make_async_remote_copy(
            src_ref=ext.at[s, dest], dst_ref=cols.at[s, me],
            send_sem=send1.at[s, k - 1], recv_sem=recv1.at[s, k - 1],
            device_id={"space": dest}, device_id_type=MESH,
        )

    def backward(s, k):
        dest = lax.rem(me + k, peers)
        return pltpu.make_async_remote_copy(
            src_ref=turned.at[s, dest], dst_ref=back.at[s, me],
            send_sem=send2.at[s, k - 1], recv_sem=recv2.at[s, k - 1],
            device_id={"space": dest}, device_id_type=MESH,
        )

    edge = lax.broadcasted_iota(jnp.int32, (8, width), 0)

    def first(s, start):
        remesh_rows(lambda z, r: q_ref[s, z, pl.ds(r, step), :])

        def store(c, total):
            swept[:, c:c + BLOCK] = total

        diffuse_rows(s, store)
        if start:
            weigh(1, wy)

        @pl.loop(0, nz * peers)
        def _(i):
            p, z = i // nz, i % nz
            lanes = pl.ds(pl.multiple_of(p * width, width), width)
            y = swept[pl.ds(pl.multiple_of(z * rows, rows), rows), lanes]
            pad = jnp.zeros((8, width), jnp.float32)
            acc = jnp.zeros((rows + 16, width), jnp.float32)
            for m in range(-2, 4):
                term = jnp.concatenate([pad, y * wy[z, m + 2, :, lanes], pad], axis=0)
                acc = acc + (term if m == 0 else pltpu.roll(term, m % (rows + 16), 0))
            ext[s, p, z, 0:rows, :] = acc[8:8 + rows]
            ext[s, p, z, rows:rows + 8, :] = jnp.where(edge < 3, acc[rows + 8:], acc[:8])

        cols[s, me] = ext[s, me]

    @pl.loop(0, 1)
    def _(s):
        first(s, True)

    for k in range(1, peers):
        forward(0, k).start()

    @pl.loop(1, ns)
    def _(s):
        first(s, False)
        for k in range(1, peers):
            forward(s, k).start()

    @pl.loop(0, ns)
    def _(s):
        for k in range(1, peers):
            forward(s, k).wait_recv()

        for p in range(peers):
            for z in range(nz):
                lanes = slice(z * width, (z + 1) * width)
                top = jnp.where(edge < 3, cols[s, (p - 1) % peers, z, rows:rows + 8, :], 0.0)
                low = jnp.where(edge >= 6, cols[s, (p + 1) % peers, z, rows:rows + 8, :], 0.0)
                at = 8 + p * rows
                tall[at:at + 8, lanes] = cols[s, p, z, 0:8, :] + top
                tall[at + 8:at + rows - 8, lanes] = cols[s, p, z, 8:rows - 8, :]
                tall[at + rows - 8:at + rows, lanes] = cols[s, p, z, rows - 8:rows, :] + low
        tall[0:8, :] = tall[ny:ny + 8, :]
        tall[ny + 8:ny + 16, :] = tall[8:16, :]

        @pl.loop(0, peers)
        def _(p):
            at = pl.multiple_of(p * rows, rows)
            ahead = REACH - sy_ref[...]
            for z in range(nz):
                lanes = slice(z * width, (z + 1) * width)
                u = tall[pl.ds(at, rows + 16), lanes]
                for bit in (1, 2, 4, 8, 16):
                    u = jnp.where((ahead & bit) != 0, pltpu.roll(u, rows + 16 - bit, 0), u)
                col_hi[pl.ds(at, rows), lanes], col_lo[pl.ds(at, rows), lanes] = halves(u[:rows])

        for a in range(by):
            total = jnp.zeros((BLOCK, nz * width), jnp.float32)
            for b in range(by):
                d = ((b - a) % by) * BLOCK
                high, low = yh_ref[s, :, d:d + BLOCK], yl_ref[s, :, d:d + BLOCK]
                left = col_hi[b * BLOCK:(b + 1) * BLOCK, :]
                rest = col_lo[b * BLOCK:(b + 1) * BLOCK, :]
                total = total + (dot32(high, left) + (dot32(low, left) + dot32(high, rest)))
            for h in range(BLOCK // rows):
                for z in range(nz):
                    turned[s, a * (BLOCK // rows) + h, z] = total[
                        h * rows:(h + 1) * rows, z * width:(z + 1) * width
                    ]
        back[s, me] = turned[s, me]
        for k in range(1, peers):
            backward(s, k).start()

    @pl.loop(0, ns)
    def _(s):
        for k in range(1, peers):
            backward(s, k).wait_recv()
        remesh_rows(
            lambda z, r: jnp.concatenate(
                [back[s, p, z, pl.ds(r, step), :] for p in range(peers)], axis=1
            )
        )

        def store(c, total):
            for z in range(nz):
                out_ref[s, z, :, c:c + BLOCK] = total[z * rows:(z + 1) * rows]

        diffuse_rows(s, store)

    @pl.loop(0, ns)
    def _(s):
        for k in range(1, peers):
            forward(s, k).wait_send()
            backward(s, k).wait_send()

    for n in range(2):
        for k in range(1, groups):
            spread(n, k).wait_send()


def sweeps_on_device(peers, groups, scalars, velocity_x, velocity_y, shift_x, shift_y, schmidt):
    ns, nz, rows, nx = scalars.shape
    ny, width = rows * peers, nx // peers
    diffusivity = jnp.exp2((3 - schmidt).astype(jnp.float32))
    line_x = jnp.roll(response(0.5 * diffusivity, nx), -(REACH + 2), axis=1)
    line_y = response(diffusivity, ny)
    xh, xl = circulant_blocks(line_x)
    yh, yl = circulant_blocks(line_y)
    f32, bf16 = jnp.float32, jnp.bfloat16
    vmem = pl.BlockSpec(memory_space=pltpu.VMEM)
    dma = pltpu.SemaphoreType.DMA((ns, peers - 1))
    return pl.pallas_call(
        functools.partial(sweeps_kernel, peers, groups),
        out_shape=jax.ShapeDtypeStruct(scalars.shape, f32),
        in_specs=[vmem] * 9,
        out_specs=vmem,
        scratch_shapes=[
            pltpu.VMEM((nz, 6, rows, nx), f32),
            pltpu.VMEM((nz, 6, rows, nx), f32),
            pltpu.VMEM((nz * rows, nx), bf16),
            pltpu.VMEM((nz * rows, nx), bf16),
            pltpu.VMEM((nz * rows, nx), f32),
            pltpu.VMEM((ny, nz * width), bf16),
            pltpu.VMEM((ny, nz * width), bf16),
            pltpu.VMEM((ny + 16, nz * width), f32),
            pltpu.VMEM((ns, peers, nz, rows + 8, width), f32),
            pltpu.VMEM((ns, peers, nz, rows + 8, width), f32),
            pltpu.VMEM((ns, peers, nz, rows, width), f32),
            pltpu.VMEM((ns, peers, nz, rows, width), f32),
            pltpu.VMEM((2, groups) + velocity_x.shape, f32),
            pltpu.SemaphoreType.DMA((2, groups - 1)),
            pltpu.SemaphoreType.DMA((2, groups - 1)),
            dma, dma, dma, dma,
        ],
        compiler_params=pltpu.CompilerParams(
            collective_id=0, has_side_effects=True, vmem_limit_bytes=62 * 2**20
        ),
    )(
        scalars, velocity_x, velocity_y, shift_x[:, :, None], shift_y[None, :], xh, xl, yh, yl
    )


def fits_kernel(mesh):
    return NY % mesh.shape["space"] == 0 and NY // mesh.shape["space"] in (128, 256)


def solution(mesh):
    peers = mesh.shape["space"]
    body = functools.partial(sweeps_on_device, peers, mesh.shape["scalar"]) if fits_kernel(mesh) else on_device
    return jax.shard_map(
        body,
        mesh=mesh,
        in_specs=(
            P("scalar", None, "space", None),
            P(None, "space", "scalar"),
            P(None, "space", "scalar"),
            P(None, "space"),
            P("space"),
            P("scalar"),
        ),
        out_specs=P("scalar", None, "space", None),
        check_vma=False,
    )
```

profile of v0, /device:TPU:31, one launch (start us, length us, event | category | flops | bytes accessed | tf_op | source)
XLA Modules:
  0.0 181.0 jit_solution(1054001675302102557)
XLA Ops:
  0.0 0.0 copy-start
  0.0 0.8 fusion.6
  0.8 0.0 copy-start.1
  0.8 2.8 %fusion = f32[4,1024]{1,0:T(4,128)S(1)} fusion(f32[513,1024]{1,0:T(8,128)} %constant.11.clone, f32[513]{0:T(1024)S(1)} %convert_multiply_fusion, f32[4]{0:T(128)S(1)} %get-tuple-element.14), kind=kOutput, calls=%fused_computation.3 | convolution fusion | flops 25219080 | bytes 2119700 | tf_op jit(solution)/shard_map/dot_general | solution.py:157
  3.6 0.1 slice.10
  3.7 0.1 pad_maximum_fusion
  3.8 0.6 broadcast_in_dim.20.g_ref
  4.4 0.0 copy-done
  4.4 1.2 fusion.1
  5.6 0.6 broadcast_in_dim.21.g_ref
  6.2 0.0 copy-done.1
  6.2 0.8 copy.9.sx_ref
  7.0 3.8 %shard_map.83 = (bf16[4,256,1024]{2,1,0:T(8,128)(2,1)}, bf16[4,256,1024]{2,1,0:T(8,128)(2,1)}) custom-call(f32[4,1,1024]{2,1,0:T(1,128)} %broadcast_in_dim.21.g_ref), custom_call_target="tpu_custom_call" | custom-call | tf_op jit(solution)/shard_map/pallas_call | solution.py:172
  10.8 3.7 %shard_map.82 = (bf16[4,256,1024]{2,1,0:T(8,128)(2,1)}, bf16[4,256,1024]{2,1,0:T(8,128)(2,1)}) custom-call(f32[4,1,1024]{2,1,0:T(1,128)} %broadcast_in_dim.20.g_ref), custom_call_target="tpu_custom_call" | custom-call | tf_op jit(solution)/shard_map/pallas_call | solution.py:172
  14.5 161.7 %shard_map.84 = f32[4,2,128,1024]{3,2,1,0:T(8,128)} custom-call(f32[4,2,128,1024]{3,2,1,0:T(8,128)} %q_ref.1, f32[2,128,256]{2,1,0:T(8,128)} %vx_ref.1, f32[2,128,256]{2,1,0:T(8,128)} %vy_ref.1, s32[2,128,1]{2,1,0:T(8,128)} %copy.9.sx_ref, s32[1,128]{1,0:T(1,128)} %bitcast.5, bf16[4,256,1024]{2,1,0:T(8,128)(2,1)} %get-tuple-element.9.xh_ref, ...), custom_call_target="tpu_custom_call" | custom-call | tf_op jit(solution)/shard_map/pallas_call | solution.py:407
  176.2 4.8 %copy.11 = f32[4,2,128,1024]{3,2,1,0:T(8,128)} copy(f32[4,2,128,1024]{3,2,1,0:T(8,128)} %shard_map.84) | data formatting | bytes 8388608
  (2 shorter events, 0.0 us)
Async XLA Ops:
  0.0 4.4 %copy-start = (f32[513,1024]{1,0:T(8,128)S(1)}, f32[513,1024]{1,0:T(8,128)}, u32[]{:S(2)}) copy-start(f32[513,1024]{1,0:T(8,128)} %constant.11.clone) | copy-start | bytes 6303748
  0.8 5.4 %copy-start.1 = (s32[2,128]{1,0:T(2,128)S(1)}, s32[2,128]{1,0:T(2,128)}, u32[]{:S(2)}) copy-start(s32[2,128]{1,0:T(2,128)} %param.11) | copy-start | bytes 3076
where the time goes:
time: 183 us; the launch traced here: 181 us
  Pallas kernels  169 us (92%)
  local copies, waits for them, and re-layouts  6.91 us (4%)
  matrix products  3.95 us (2%)
    pallas_call x1, Pallas kernels, sweeps_on_device(): pl.pallas_call(functools.partial(sweeps_kernel, peers, groups), out_shape...  162 us
    pallas_call x2, Pallas kernels, circulant_blocks(): pl.pallas_call(circulant_kernel, grid=(count,), in_specs=[pl.BlockSpec((1...  7.56 us
    unnamed x5, local copies, waits for them, and re-layouts  4.8 us
    dot_general x2, matrix products, response(): jnp.dot(damping, table, precision=lax.Precision.HIGHEST, preferred_elemen...  3.95 us

commit v1 on v0

v1 whole, which is shorter than its diff:
```python
import functools
import math

import jax
import jax.numpy as jnp
import numpy as np
from jax import lax
from jax.experimental import pallas as pl
from jax.experimental.pallas import tpu as pltpu
from jax.sharding import PartitionSpec as P

NY = 1024


def spline(distance):
    magnitude = jnp.abs(distance)
    far_part = jnp.maximum(3.0 - magnitude, 0.0)
    middle = jnp.maximum(2.0 - magnitude, 0.0)
    near_part = jnp.maximum(1.0 - magnitude, 0.0)
    return (far_part**5 - 6.0 * middle**5 + 15.0 * near_part**5) / 120.0


def remesh(fields, fraction, shift_line):
    summed = jnp.zeros_like(fields)
    for offset in range(-2, 4):
        weight = spline(offset - fraction)
        summed = summed + jnp.roll(fields * weight, offset, axis=-1)
    line_shift = shift_line[None, :, :, None]
    moved = summed
    for amount in range(-8, 9):
        moved = jnp.where(line_shift == amount, jnp.roll(summed, amount, axis=-1), moved)
    return moved


def remesh_columns(fields, fraction, shift_cols):
    summed = jnp.zeros_like(fields)
    for offset in range(-2, 4):
        weight = spline(offset - fraction)
        summed = summed + jnp.roll(fields * weight[None], offset, axis=2)
    column_shift = shift_cols[None, None, None, :]
    moved = summed
    for amount in range(-8, 9):
        moved = jnp.where(column_shift == amount, jnp.roll(summed, amount, axis=2), moved)
    return moved


def spectral_tables(length):
    midpoint = length // 2
    column = jnp.arange(length, dtype=jnp.int32)
    wavenum = jnp.where(column <= midpoint, column, column - midpoint)
    phases = column[:, None] * wavenum[None, :] % length
    angles = phases.astype(jnp.float32) * (2.0 * math.pi / length)
    forward = jnp.where((column <= midpoint)[None, :], jnp.cos(angles), jnp.sin(angles))
    inverse_weight = jnp.where((wavenum == 0) | (column == midpoint), 1.0, 2.0) / length
    inverse = forward.T * inverse_weight[:, None]
    relative = wavenum.astype(jnp.float32) / midpoint
    return (forward, inverse, relative * relative)


def diffuse(fields, diffusivity, tables):
    forward, inverse, wave_square = tables
    initial = fields.shape
    rows_flat = fields.reshape(-1, initial[-1])
    spectra = jnp.dot(
        rows_flat, forward, precision=lax.Precision.HIGHEST, preferred_element_type=jnp.float32
    )
    damping = jnp.exp(-diffusivity[:, None] * wave_square[None, :])
    spectra = spectra.reshape(initial) * damping[:, None, None, :]
    result = jnp.dot(
        spectra.reshape(-1, initial[-1]),
        inverse,
        precision=lax.Precision.HIGHEST,
        preferred_element_type=jnp.float32,
    )
    return result.reshape(initial)


def diffuse_columns(fields, diffusivity, tables):
    forward, inverse, wave_square = tables
    spectra = jnp.einsum(
        "jk,szjx->szkx",
        forward,
        fields,
        precision=lax.Precision.HIGHEST,
        preferred_element_type=jnp.float32,
    )
    damping = jnp.exp(-diffusivity[:, None] * wave_square[None, :])
    spectra = spectra * damping[:, None, :, None]
    return jnp.einsum(
        "kj,szkx->szjx",
        inverse,
        spectra,
        precision=lax.Precision.HIGHEST,
        preferred_element_type=jnp.float32,
    )


def one_sweep(fields, fraction, shift_line, diffusivity, tables):
    return diffuse(remesh(fields, fraction, shift_line), diffusivity, tables)


def fetch_velocity(velocity_x):
    return lax.all_gather(velocity_x, "scalar", axis=2, tiled=True)


def on_device(scalars, velocity_x, velocity_y, shift_x, shift_y, schmidt):
    diffusivity = jnp.exp2((3 - schmidt).astype(jnp.float32))
    tables_x = spectral_tables(scalars.shape[3])
    tables_y = spectral_tables(NY)
    along_x = fetch_velocity(velocity_x)
    fields = one_sweep(scalars, along_x, shift_x, 0.5 * diffusivity, tables_x)
    along_y = lax.all_gather(velocity_y, "scalar", axis=2, tiled=True)
    fields_cols, velocity_cols = (
        lax.all_to_all(fields, "space", split_axis=3, concat_axis=2, tiled=True),
        lax.all_to_all(along_y[None], "space", split_axis=3, concat_axis=2, tiled=True),
    )
    remeshed = remesh_columns(fields_cols, velocity_cols[0], shift_y)
    returned = diffuse_columns(remeshed, diffusivity, tables_y)
    fields = lax.all_to_all(returned, "space", split_axis=2, concat_axis=3, tiled=True)
    along_x = fetch_velocity(velocity_x)
    return one_sweep(fields, along_x, shift_x, 0.5 * diffusivity, tables_x)


BLOCK = 256
REACH = 8
MESH = pl.DeviceIdType.MESH


def spline_weights(f):
    g = 1.0 - f

    def fifth(v):
        w = v * v
        return w * w * v

    f0, f1, f2 = fifth(f), fifth(1.0 + f), fifth(2.0 + f)
    g0, g1, g2 = fifth(g), fifth(1.0 + g), fifth(2.0 + g)
    c = 1.0 / 120.0
    return (
        g0 * c,
        (g1 - 6.0 * g0) * c,
        (g2 - 6.0 * g1 + 15.0 * g0) * c,
        (f2 - 6.0 * f1 + 15.0 * f0) * c,
        (f1 - 6.0 * f0) * c,
        f0 * c,
    )


STEP = 16
LANES = 128


def cosine_table(length):
    half = length // 2
    k = np.arange(half)
    weight = np.where(k == 0, 1.0, 2.0) / length
    phase = (k[:, None] * np.arange(length)[None, :]) % length
    return (np.cos(phase * (2.0 * np.pi / length)) * weight[:, None]).astype(np.float32)


def halves(v):
    high = v.astype(jnp.bfloat16)
    return high, (v - high.astype(jnp.float32)).astype(jnp.bfloat16)


def dot32(a, b):
    return jnp.dot(a, b, preferred_element_type=jnp.float32)


def transport_kernel(
    peers, groups,
    q_hbm, vx_ref, vy_ref, sx_ref, sy_ref, sc_ref, cos_hbm,
    out_ref,
    q_ref, cos_ref, line, th, tl, shift_of, place_of, wx, wy, part_hi, part_lo,
    ext, cols, col_hi, col_lo, turned, back, held, colv,
    sem_q, sem_c, sendx, recvx, sendv, recvv, send_up, send_down, recv_relay,
    send1, recv1, send2, recv2,
):
    ns, nz, rows, nx = q_ref.shape
    ny = rows * peers
    width = nx // peers
    ratio = peers // groups
    bx, by = nx // BLOCK, ny // BLOCK
    me = lax.axis_index("space")
    mine = lax.axis_index("scalar")
    home = me // ratio
    half = rows // 2
    parts = ((0, 0, half), (0, half, half), (1, 0, rows))

    def load(s, z):
        return pltpu.make_async_copy(q_hbm.at[s, z], q_ref.at[s, z], sem_q.at[s, z])

    tables = pltpu.make_async_copy(cos_hbm, cos_ref, sem_c)
    tables.start()
    for z in range(nz):
        for s in range(ns):
            load(s, z).start()

    barrier = pltpu.get_barrier_semaphore()
    for k in range(1, peers):
        pl.semaphore_signal(barrier, inc=1, device_id={"space": lax.rem(me + k, peers)}, device_id_type=MESH)
    for k in range(1, groups):
        pl.semaphore_signal(barrier, inc=1, device_id={"scalar": lax.rem(mine + k, groups)}, device_id_type=MESH)
    pl.semaphore_wait(barrier, peers + groups - 2)

    def spread(c, k):
        z, r, n = parts[c]
        return pltpu.make_async_remote_copy(
            src_ref=vx_ref.at[z, pl.ds(r, n), :], dst_ref=held.at[mine, z, pl.ds(r, n), :],
            send_sem=sendx.at[c, k - 1], recv_sem=recvx.at[c, k - 1],
            device_id={"scalar": lax.rem(mine + k, groups)}, device_id_type=MESH,
        )

    def collect(z, h):
        dest = ratio * mine + h
        k = lax.rem(dest - me + peers, peers)
        return pltpu.make_async_remote_copy(
            src_ref=vy_ref.at[z, :, pl.ds(h * width, width)], dst_ref=colv.at[z, me],
            send_sem=sendv.at[z, h], recv_sem=recvv.at[z, k],
            device_id={"space": dest}, device_id_type=MESH,
        )

    def collected(z, k):
        return pltpu.make_async_remote_copy(
            src_ref=vy_ref.at[z, :, pl.ds(0, width)], dst_ref=colv.at[z, me],
            send_sem=sendv.at[z, 0], recv_sem=recvv.at[z, k],
            device_id={"space": lax.rem(me + k, peers)}, device_id_type=MESH,
        )

    def relay(j, up):
        z, i = j // (peers // 2), j % (peers // 2)
        block = colv.at[z, pl.ds(2 * i, 2)]
        return pltpu.make_async_remote_copy(
            src_ref=block, dst_ref=block,
            send_sem=(send_up if up else send_down).at[j], recv_sem=recv_relay.at[j],
            device_id={"scalar": lax.rem(mine + (1 if up else groups - 1), groups)}, device_id_type=MESH,
        )

    goes_up = jnp.logical_and(mine >= home, mine < groups - 1)
    goes_down = jnp.logical_and(mine <= home, mine > 0)

    def pass_on(j):
        @pl.when(goes_up)
        def _():
            relay(j, True).start()

        @pl.when(goes_down)
        def _():
            relay(j, False).start()

    for k in range(1, groups):
        spread(0, k).start()
    for z in range(nz):
        for h in range(ratio):
            @pl.when(ratio * mine + h != me)
            def _():
                collect(z, h).start()

            @pl.when(ratio * mine + h == me)
            def _():
                colv[z, me] = vy_ref[z, :, h * width:(h + 1) * width]
    for c in range(1, len(parts)):
        for k in range(1, groups):
            spread(c, k).start()
    held[mine] = vx_ref[...]

    lane = lax.broadcasted_iota(jnp.int32, (rows, LANES), 1)
    for z in range(nz):
        shift = jnp.transpose(jnp.broadcast_to(sx_ref[z:z + 1, :] + REACH, (LANES, rows)))
        shift_of[z] = shift
        place_of[z] = (lane - shift) & (LANES - 1)

    top = nx // 2
    row = lax.broadcasted_iota(jnp.int32, (2 * ns, top), 0)
    index = jnp.full((2 * ns, top), sc_ref[0], jnp.int32)
    for s in range(1, ns):
        index = jnp.where(row % ns == s, sc_ref[s], index)
    rate = jnp.exp2((3 - index).astype(jnp.float32))
    rate = jnp.where(row < ns, 0.5 * rate, rate)
    relative = lax.broadcasted_iota(jnp.int32, (2 * ns, top), 1).astype(jnp.float32) / top
    damping = jnp.exp(-rate * relative * relative)
    tables.wait()
    g = jnp.dot(damping, cos_ref[...], precision=lax.Precision.HIGHEST, preferred_element_type=jnp.float32)
    last = jnp.exp(-rate[:, 0:1]) / nx
    odd = lax.broadcasted_iota(jnp.int32, (2 * ns, nx), 1) % 2
    g = g + jnp.where(odd == 1, -last, last)
    line[0:ns, :] = pltpu.roll(g, nx - (REACH + 2), 1)[0:ns]
    line[ns:, :] = pltpu.roll(g, REACH + 2, 1)[ns:]

    def circulant(t):
        for r in range(0, BLOCK, 64):
            wide = jnp.broadcast_to(line[pl.ds(t, 1), :], (64, nx))
            wide = pltpu.roll(wide, r, 1, stride=1, stride_axis=0)
            th[t, r:r + 64, :], tl[t, r:r + 64, :] = halves(wide)

    pl.loop(0, ns)(circulant)

    def weigh_rows(c):
        z, first_row, n = parts[c]
        for k in range(1, groups):
            spread(c, k).wait_recv()

        @pl.loop(0, n // 8)
        def _(i):
            at = pl.ds(pl.multiple_of(first_row + i * 8, 8), 8)
            f = jnp.concatenate([held[g, z, at, :] for g in range(groups)], axis=1)
            for m, w in enumerate(spline_weights(f)):
                wx[z, m, at, :] = pltpu.roll(w, m % 3, 1) if m % 3 else w

    def remesh_eight(z, at, q):
        one, two = pltpu.roll(q, 1, 1), pltpu.roll(q, 2, 1)
        near = q * wx[z, 0, at, :] + one * wx[z, 1, at, :] + two * wx[z, 2, at, :]
        far = q * wx[z, 3, at, :] + one * wx[z, 4, at, :] + two * wx[z, 5, at, :]
        total = near + pltpu.roll(far, 3, 1)
        place, shift = place_of[z, at, :], shift_of[z, at, :]
        stays = lax.broadcasted_iota(jnp.int32, shift.shape, 1) >= shift
        moved = [
            jnp.take_along_axis(total[:, v:v + LANES], place, axis=1) for v in range(0, nx, LANES)
        ]
        return jnp.concatenate(
            [jnp.where(stays, moved[v], moved[v - 1]) for v in range(nx // LANES)], axis=1
        )

    def remesh_rows(z, first_row, n, read):
        @pl.loop(0, n // STEP, unroll=2)
        def _(i):
            r = pl.multiple_of(first_row + i * STEP, STEP)
            both = [
                remesh_eight(z, pl.ds(pl.multiple_of(r + e, 8), 8), read(pl.ds(pl.multiple_of(r + e, 8), 8)))
                for e in (0, 8)
            ]
            at = pl.ds(r, STEP)
            part_hi[at, :], part_lo[at, :] = halves(jnp.concatenate(both, axis=0))

    def diffuse_rows(s, first_row, n, store):
        at = slice(first_row, first_row + n)
        for b in range(bx):
            total = jnp.zeros((n, BLOCK), jnp.float32)
            for a in range(bx):
                d = ((b - a) % bx) * BLOCK
                high, low = th[s, :, d:d + BLOCK], tl[s, :, d:d + BLOCK]
                left = part_hi[at, a * BLOCK:(a + 1) * BLOCK]
                rest = part_lo[at, a * BLOCK:(a + 1) * BLOCK]
                total = total + (dot32(left, high) + (dot32(left, low) + dot32(rest, high)))
            store(b, total)

    def forward(s, c, k):
        z, r, n = parts[c]
        dest = lax.rem(me + k, peers)
        return pltpu.make_async_remote_copy(
            src_ref=ext.at[s, z, dest, pl.ds(r, n), :], dst_ref=cols.at[s, z, me, pl.ds(r, n), :],
            send_sem=send1.at[s, c, k - 1], recv_sem=recv1.at[s, c, k - 1],
            device_id={"space": dest}, device_id_type=MESH,
        )

    def backward(s, z, k):
        dest = lax.rem(me + k, peers)
        return pltpu.make_async_remote_copy(
            src_ref=turned.at[s, dest, z], dst_ref=back.at[s, me, z],
            send_sem=send2.at[s, z, k - 1], recv_sem=recv2.at[s, z, k - 1],
            device_id={"space": dest}, device_id_type=MESH,
        )

    per = BLOCK // width

    def first_sweep(s, c):
        z, r, n = parts[c]
        remesh_rows(z, r, n, lambda at: q_ref[s, z, at, :])

        def store(b, total):
            for h in range(per):
                ext[s, z, b * per + h, r:r + n, :] = total[:, h * width:(h + 1) * width]

        diffuse_rows(s, r, n, store)
        for k in range(1, peers):
            forward(s, c, k).start()
        cols[s, z, me, r:r + n, :] = ext[s, z, me, r:r + n, :]

    def await_relay(j):
        @pl.when(mine != home)
        def _():
            relay(j, True).wait_recv()
            pass_on(j)

    count = nz * peers // 2
    for c in range(len(parts)):
        weigh_rows(c)

        @pl.loop(0, ns)
        def _(s):
            if parts[c][1] == 0:
                load(s, parts[c][0]).wait()
            first_sweep(s, c)
            if c == len(parts) - 1:
                await_relay(s)

        if c == 0:
            @pl.when(mine == home)
            def _():
                for z in range(nz):
                    for k in range(1, peers):
                        collected(z, k).wait_recv()

                    @pl.loop(z * (peers // 2), (z + 1) * (peers // 2))
                    def _(j):
                        pass_on(j)

    reach = 24
    part = 64

    def weigh_columns(z):
        @pl.loop(0, ny // part)
        def _(i):
            y = i * part
            before = lax.rem(y - 8 + ny, ny)
            f = jnp.concatenate(
                [
                    colv[z, before // rows, pl.ds(pl.multiple_of(before % rows, 8), 8), :],
                    colv[z, y // rows, pl.ds(pl.multiple_of(y % rows, part), part), :],
                ],
                axis=0,
            )
            for m, w in enumerate(spline_weights(f)):
                w = pltpu.roll(w, m % 3, 0) if m % 3 else w
                wy[z, m, pl.ds(pl.multiple_of(reach + y, 8), part), :] = w[8:]

        for m in range(6):
            wy[z, m, 0:reach, :] = wy[z, m, ny:ny + reach, :]

    @pl.loop(ns, count)
    def _(j):
        circulant(j)
        await_relay(j)

    for t in range(count, 2 * ns):
        circulant(t)
    for z in range(nz):
        weigh_columns(z)

    @pl.loop(0, ns)
    def _(s):
        for c in range(len(parts)):
            for k in range(1, peers):
                forward(s, c, k).wait_recv()

        @pl.loop(0, ny // part)
        def _(i):
            y = i * part
            before = lax.rem(y - reach + ny, ny)
            shift = sy_ref[...] + REACH
            for z in range(nz):
                q = jnp.concatenate(
                    [
                        cols[s, z, before // rows, pl.ds(pl.multiple_of(before % rows, 8), reach), :],
                        cols[s, z, y // rows, pl.ds(pl.multiple_of(y % rows, part), part), :],
                    ],
                    axis=0,
                )
                at = pl.ds(pl.multiple_of(y, part), reach + part)
                one, two = pltpu.roll(q, 1, 0), pltpu.roll(q, 2, 0)
                near = q * wy[z, 0, at, :] + one * wy[z, 1, at, :] + two * wy[z, 2, at, :]
                far = q * wy[z, 3, at, :] + one * wy[z, 4, at, :] + two * wy[z, 5, at, :]
                u = near + pltpu.roll(far, 3, 0)
                for bit in (1, 2, 4, 8, 16):
                    u = jnp.where((shift & bit) != 0, pltpu.roll(u, bit, 0), u)
                put = pl.ds(pl.multiple_of(y, part), part)
                lanes = slice(z * width, (z + 1) * width)
                col_hi[put, lanes], col_lo[put, lanes] = halves(u[reach:])

        for a in range(by):
            total = jnp.zeros((BLOCK, nz * width), jnp.float32)
            for b in range(by):
                d = ((b - a) % by) * BLOCK
                high, low = th[ns + s, :, d:d + BLOCK], tl[ns + s, :, d:d + BLOCK]
                left = col_hi[b * BLOCK:(b + 1) * BLOCK, :]
                rest = col_lo[b * BLOCK:(b + 1) * BLOCK, :]
                total = total + (dot32(high, left) + (dot32(low, left) + dot32(high, rest)))
            for h in range(BLOCK // rows):
                for z in range(nz):
                    turned[s, a * (BLOCK // rows) + h, z] = total[
                        h * rows:(h + 1) * rows, z * width:(z + 1) * width
                    ]
        for z in range(nz):
            for k in range(1, peers):
                backward(s, z, k).start()
        back[s, me] = turned[s, me]

    @pl.loop(0, ns)
    def _(s):
        for z in range(nz):
            for k in range(1, peers):
                backward(s, z, k).wait_recv()
            remesh_rows(
                z, 0, rows,
                lambda at: jnp.concatenate([back[s, p, z, at, :] for p in range(peers)], axis=1),
            )

            def store(b, total):
                out_ref[s, z, :, b * BLOCK:(b + 1) * BLOCK] = total

            diffuse_rows(s, 0, rows, store)

    @pl.loop(0, ns)
    def _(s):
        for k in range(1, peers):
            for c in range(len(parts)):
                forward(s, c, k).wait_send()
            for z in range(nz):
                backward(s, z, k).wait_send()

    for c in range(len(parts)):
        for k in range(1, groups):
            spread(c, k).wait_send()
    for z in range(nz):
        for h in range(ratio):
            @pl.when(ratio * mine + h != me)
            def _():
                collect(z, h).wait_send()

    @pl.loop(0, count)
    def _(j):
        @pl.when(goes_up)
        def _():
            relay(j, True).wait_send()

        @pl.when(goes_down)
        def _():
            relay(j, False).wait_send()


def transport_on_device(peers, groups, scalars, velocity_x, velocity_y, shift_x, shift_y, schmidt):
    ns, nz, rows, nx = scalars.shape
    ny, width = rows * peers, nx // peers
    f32, bf16, i32 = jnp.float32, jnp.bfloat16, jnp.int32
    vmem = pl.BlockSpec(memory_space=pltpu.VMEM)
    smem = pl.BlockSpec(memory_space=pltpu.SMEM)
    anywhere = pl.BlockSpec(memory_space=pl.ANY)
    count = nz * peers // 2
    dma = pltpu.SemaphoreType.DMA
    return pl.pallas_call(
        functools.partial(transport_kernel, peers, groups),
        out_shape=jax.ShapeDtypeStruct(scalars.shape, f32),
        in_specs=[anywhere, vmem, vmem, vmem, vmem, smem, anywhere],
        out_specs=vmem,
        scratch_shapes=[
            pltpu.VMEM(scalars.shape, f32),
            pltpu.VMEM((nx // 2, nx), f32),
            pltpu.VMEM((2 * ns, nx), f32),
            pltpu.VMEM((2 * ns, BLOCK, nx), bf16),
            pltpu.VMEM((2 * ns, BLOCK, nx), bf16),
            pltpu.VMEM((nz, rows, LANES), i32),
            pltpu.VMEM((nz, rows, LANES), i32),
            pltpu.VMEM((nz, 6, rows, nx), f32),
            pltpu.VMEM((nz, 6, ny + 24, width), f32),
            pltpu.VMEM((rows, nx), bf16),
            pltpu.VMEM((rows, nx), bf16),
            pltpu.VMEM((ns, nz, peers, rows, width), f32),
            pltpu.VMEM((ns, nz, peers, rows, width), f32),
            pltpu.VMEM((ny, nz * width), bf16),
            pltpu.VMEM((ny, nz * width), bf16),
            pltpu.VMEM((ns, peers, nz, rows, width), f32),
            pltpu.VMEM((ns, peers, nz, rows, width), f32),
            pltpu.VMEM((groups,) + velocity_x.shape, f32),
            pltpu.VMEM((nz, peers, rows, width), f32),
            dma((ns, nz)),
            dma,
            dma((3, groups - 1)),
            dma((3, groups - 1)),
            dma((nz, peers // groups)),
            dma((nz, peers)),
            dma((count,)),
            dma((count,)),
            dma((count,)),
            dma((ns, 3, peers - 1)),
            dma((ns, 3, peers - 1)),
            dma((ns, nz, peers - 1)),
            dma((ns, nz, peers - 1)),
        ],
        compiler_params=pltpu.CompilerParams(
            collective_id=0, has_side_effects=True, vmem_limit_bytes=60 * 2**20
        ),
    )(
        scalars, velocity_x, velocity_y, shift_x, shift_y[None, :], schmidt,
        jnp.asarray(cosine_table(nx)),
    )


def transport(peers, groups, scalars, *others):
    ns, nz, rows, nx = scalars.shape
    fits = (
        peers % groups == 0 and peers % 2 == 0 and nz == 2 and rows == LANES and nx == rows * peers == NY
        and ns <= nz * peers // 2 and others[0].shape[2] == nx // groups and nx % BLOCK == 0
    )
    if not fits:
        return on_device(scalars, *others)
    return transport_on_device(peers, groups, scalars, *others)


def solution(mesh):
    peers = mesh.shape["space"]
    body = functools.partial(transport, peers, mesh.shape["scalar"])
    return jax.shard_map(
        body,
        mesh=mesh,
        in_specs=(
            P("scalar", None, "space", None),
            P(None, "space", "scalar"),
            P(None, "space", "scalar"),
            P(None, "space"),
            P("space"),
            P("scalar"),
        ),
        out_specs=P("scalar", None, "space", None),
        check_vma=False,
    )
```

time: 183 us -> 127 us (0.69)
  Pallas kernels: 169 us -> 122 us
  matrix products: 3.95 us -> 0 us
  local copies, waits for them, and re-layouts: 6.91 us -> 4.79 us
    pallas_call x3 -> x1, Pallas kernels: 169 us -> 122 us  [transport_on_device(): pl.pallas_call(functools.partial(transport_kernel, peers, groups), out_sh...]
    dot_general x2 -> x0, matrix products: 3.95 us -> none  [response(): jnp.dot(damping, table, precision=lax.Precision.HIGHEST, preferred_elemen...]
    broadcast_in_dim x3 -> x0, local copies, waits for them, and re-layouts: 2.03 us -> none  [the longest x2 1.24 us: circulant_blocks(): g[:, None, :]]
    unnamed x5 -> x1, local copies, waits for them, and re-layouts: 4.8 us -> 4.79 us
where the time goes in v1:
time: 127 us
  Pallas kernels  122 us (96%)
  local copies, waits for them, and re-layouts  4.79 us (4%)
    pallas_call x1, Pallas kernels, transport_on_device(): pl.pallas_call(functools.partial(transport_kernel, peers, groups), out_sh...  122 us
    unnamed x1, local copies, waits for them, and re-layouts  4.79 us

profile of v1, /device:TPU:31, one launch (start us, length us, event | category | flops | bytes accessed | tf_op | source)
XLA Modules:
  0.0 126.6 jit_solution(8584466440625480729)
XLA Ops:
  0.0 121.8 %shard_map.73 = f32[4,2,128,1024]{3,2,1,0:T(8,128)} custom-call(f32[4,2,128,1024]{3,2,1,0:T(8,128)} %q_hbm.1, f32[2,128,256]{2,1,0:T(8,128)} %vx_ref.1, f32[2,128,256]{2,1,0:T(8,128)} %vy_ref.1, s32[2,128]{1,0:T(2,128)} %sx_ref.1, s32[1,128]{1,0:T(1,128)} %bitcast.1, s32[4]{0:T(128)} %sc_ref.1, f32[512,1024]{1,0:T(8,128)} %constant.2.clone.cos_hbm), custom_call_target="tpu_custom_call" | custom-call | tf_op jit(solution)/shard_map/pallas_call | solution.py:540
  121.8 4.8 %copy.9 = f32[4,2,128,1024]{3,2,1,0:T(8,128)} copy(f32[4,2,128,1024]{3,2,1,0:T(8,128)} %shard_map.73) | data formatting | bytes 8388608

commit v2 on v1

--- a/solution.py
+++ b/solution.py
@@ -288,19 +288,23 @@
     line[ns:, :] = pltpu.roll(g, REACH + 2, 1)[ns:]
 
     def circulant(t):
-        for r in range(0, BLOCK, 64):
+        for r in range(0, LANES, 64):
             wide = jnp.broadcast_to(line[pl.ds(t, 1), :], (64, nx))
-            wide = pltpu.roll(wide, r, 1, stride=1, stride_axis=0)
-            th[t, r:r + 64, :], tl[t, r:r + 64, :] = halves(wide)
-
-    pl.loop(0, ns)(circulant)
+            high, low = halves(pltpu.roll(wide, r, 1, stride=1, stride_axis=0))
+            for e in range(0, BLOCK, LANES):
+                at = slice(r + e, r + e + 64)
+                th[t, at, e:], tl[t, at, e:] = high[:, :nx - e], low[:, :nx - e]
+                if e:
+                    th[t, at, :e], tl[t, at, :e] = high[:, nx - e:], low[:, nx - e:]
+
+    circulant(0)
 
     def weigh_rows(c):
         z, first_row, n = parts[c]
         for k in range(1, groups):
             spread(c, k).wait_recv()
 
-        @pl.loop(0, n // 8)
+        @pl.loop(0, n // 8, unroll=2)
         def _(i):
             at = pl.ds(pl.multiple_of(first_row + i * 8, 8), 8)
             f = jnp.concatenate([held[g, z, at, :] for g in range(groups)], axis=1)
@@ -335,14 +339,12 @@
     def diffuse_rows(s, first_row, n, store):
         at = slice(first_row, first_row + n)
         for b in range(bx):
-            total = jnp.zeros((n, BLOCK), jnp.float32)
-            for a in range(bx):
-                d = ((b - a) % bx) * BLOCK
-                high, low = th[s, :, d:d + BLOCK], tl[s, :, d:d + BLOCK]
-                left = part_hi[at, a * BLOCK:(a + 1) * BLOCK]
-                rest = part_lo[at, a * BLOCK:(a + 1) * BLOCK]
-                total = total + (dot32(left, high) + (dot32(left, low) + dot32(rest, high)))
-            store(b, total)
+            turns = [((b - a) % bx) * BLOCK for a in range(bx)]
+            high = jnp.concatenate([th[s, :, d:d + BLOCK] for d in turns], axis=0)
+            low = jnp.concatenate([tl[s, :, d:d + BLOCK] for d in turns], axis=0)
+            left = part_hi[at, :]
+            both = dot32(jnp.concatenate([left, part_lo[at, :]], axis=0), high)
+            store(b, both[:n] + (dot32(left, low) + both[n:]))
 
     def forward(s, c, k):
         z, r, n = parts[c]
@@ -391,6 +393,8 @@
             if parts[c][1] == 0:
                 load(s, parts[c][0]).wait()
             first_sweep(s, c)
+            if c == 0:
+                circulant(s + 1)
             if c == len(parts) - 1:
                 await_relay(s)
 
@@ -427,14 +431,19 @@
         for m in range(6):
             wy[z, m, 0:reach, :] = wy[z, m, ny:ny + reach, :]
 
+    weigh_columns(0)
+
     @pl.loop(ns, count)
     def _(j):
-        circulant(j)
         await_relay(j)
 
-    for t in range(count, 2 * ns):
+        @pl.when(j < 2 * ns - 1)
+        def _():
+            circulant(j + 1)
+
+    for t in range(count + 1, 2 * ns):
         circulant(t)
-    for z in range(nz):
+    for z in range(1, nz):
         weigh_columns(z)
 
     @pl.loop(0, ns)
@@ -528,6 +537,16 @@
             relay(j, False).wait_send()
 
 
+def hand_over_kernel(held_ref, out_ref, sem):
+    copies = [
+        pltpu.make_async_copy(held_ref.at[s], out_ref.at[s], sem.at[s]) for s in range(held_ref.shape[0])
+    ]
+    for copy in copies:
+        copy.start()
+    for copy in copies:
+        copy.wait()
+
+
 def transport_on_device(peers, groups, scalars, velocity_x, velocity_y, shift_x, shift_y, schmidt):
     ns, nz, rows, nx = scalars.shape
     ny, width = rows * peers, nx // peers
@@ -537,9 +556,9 @@
     anywhere = pl.BlockSpec(memory_space=pl.ANY)
     count = nz * peers // 2
     dma = pltpu.SemaphoreType.DMA
-    return pl.pallas_call(
+    result = pl.pallas_call(
         functools.partial(transport_kernel, peers, groups),
-        out_shape=jax.ShapeDtypeStruct(scalars.shape, f32),
+        out_shape=pltpu.VMEM(scalars.shape, f32),
         in_specs=[anywhere, vmem, vmem, vmem, vmem, smem, anywhere],
         out_specs=vmem,
         scratch_shapes=[
@@ -577,12 +596,20 @@
             dma((ns, nz, peers - 1)),
         ],
         compiler_params=pltpu.CompilerParams(
-            collective_id=0, has_side_effects=True, vmem_limit_bytes=60 * 2**20
+            collective_id=0, has_side_effects=True, vmem_limit_bytes=52 * 2**20
         ),
     )(
         scalars, velocity_x, velocity_y, shift_x, shift_y[None, :], schmidt,
         jnp.asarray(cosine_table(nx)),
     )
+    return pl.pallas_call(
+        hand_over_kernel,
+        out_shape=jax.ShapeDtypeStruct(scalars.shape, f32),
+        in_specs=[anywhere],
+        out_specs=anywhere,
+        scratch_shapes=[dma((ns,))],
+        compiler_params=pltpu.CompilerParams(vmem_limit_bytes=2**20),
+    )(result)
 
 
 def transport(peers, groups, scalars, *others):

time: 127 us -> 118 us (0.929)
  local copies, waits for them, and re-layouts: 4.79 us -> 0 us
  Pallas kernels: 122 us -> 118 us
    pallas_call x1, Pallas kernels: 122 us -> 116 us  [transport_on_device(): pl.pallas_call(functools.partial(transport_kernel, peers, groups), out_sh...]
    unnamed x1 -> x0, local copies, waits for them, and re-layouts: 4.79 us -> none
    pallas_call x0 -> x1, Pallas kernels: none -> 2.04 us  [transport_on_device(): pl.pallas_call(hand_over_kernel, out_shape=jax.ShapeDtypeStruct(scalars.s...]
where the time goes in v2:
time: 118 us
  Pallas kernels  118 us (100%)
    pallas_call x1, Pallas kernels, transport_on_device(): pl.pallas_call(functools.partial(transport_kernel, peers, groups), out_sh...  116 us

profile of v2, /device:TPU:31, one launch (start us, length us, event | category | flops | bytes accessed | tf_op | source)
XLA Modules:
  0.0 118.2 jit_solution(454089913355227049)
XLA Ops:
  0.0 116.2 %shard_map.73.held_ref = f32[4,2,128,1024]{3,2,1,0:T(8,128)S(1)} custom-call(f32[4,2,128,1024]{3,2,1,0:T(8,128)} %q_hbm.1, f32[2,128,256]{2,1,0:T(8,128)} %vx_ref.1, f32[2,128,256]{2,1,0:T(8,128)} %vy_ref.1, s32[2,128]{1,0:T(2,128)} %sx_ref.1, s32[1,128]{1,0:T(1,128)} %bitcast.1, s32[4]{0:T(128)} %sc_ref.1, f32[512,1024]{1,0:T(8,128)} %constant.2.clone.cos_hbm), custom_call_target="tpu_custom_call" | custom-call | tf_op jit(solution)/shard_map/pallas_call | solution.py:559
  116.2 2.0 %shard_map.74 = f32[4,2,128,1024]{3,2,1,0:T(8,128)} custom-call(f32[4,2,128,1024]{3,2,1,0:T(8,128)S(1)} %shard_map.73.held_ref), custom_call_target="tpu_custom_call" | custom-call | tf_op jit(solution)/shard_map/pallas_call | solution.py:605

commit v3 on v2

--- a/solution.py
+++ b/solution.py
@@ -167,11 +167,23 @@
     return jnp.dot(a, b, preferred_element_type=jnp.float32)
 
 
+def diffuse_rows(part_hi, part_lo, th, tl, s, first_row, n, store):
+    at = slice(first_row, first_row + n)
+    blocks = part_hi.shape[1] // BLOCK
+    for b in range(blocks):
+        turns = [((b - a) % blocks) * BLOCK for a in range(blocks)]
+        high = jnp.concatenate([th[s, :, d:d + BLOCK] for d in turns], axis=0)
+        low = jnp.concatenate([tl[s, :, d:d + BLOCK] for d in turns], axis=0)
+        left = part_hi[at, :]
+        both = dot32(jnp.concatenate([left, part_lo[at, :]], axis=0), high)
+        store(b, both[:n] + (dot32(left, low) + both[n:]))
+
+
 def transport_kernel(
     peers, groups,
     q_hbm, vx_ref, vy_ref, sx_ref, sy_ref, sc_ref, cos_hbm,
-    out_ref,
-    q_ref, cos_ref, line, th, tl, shift_of, place_of, wx, wy, part_hi, part_lo,
+    out_ref, th, tl, part_hi, part_lo,
+    q_ref, cos_ref, line, shift_of, place_of, wx, wy,
     ext, cols, col_hi, col_lo, turned, back, held, colv,
     sem_q, sem_c, sendx, recvx, sendv, recvv, send_up, send_down, recv_relay,
     send1, recv1, send2, recv2,
@@ -336,16 +348,6 @@
             at = pl.ds(r, STEP)
             part_hi[at, :], part_lo[at, :] = halves(jnp.concatenate(both, axis=0))
 
-    def diffuse_rows(s, first_row, n, store):
-        at = slice(first_row, first_row + n)
-        for b in range(bx):
-            turns = [((b - a) % bx) * BLOCK for a in range(bx)]
-            high = jnp.concatenate([th[s, :, d:d + BLOCK] for d in turns], axis=0)
-            low = jnp.concatenate([tl[s, :, d:d + BLOCK] for d in turns], axis=0)
-            left = part_hi[at, :]
-            both = dot32(jnp.concatenate([left, part_lo[at, :]], axis=0), high)
-            store(b, both[:n] + (dot32(left, low) + both[n:]))
-
     def forward(s, c, k):
         z, r, n = parts[c]
         dest = lax.rem(me + k, peers)
@@ -373,7 +375,7 @@
             for h in range(per):
                 ext[s, z, b * per + h, r:r + n, :] = total[:, h * width:(h + 1) * width]
 
-        diffuse_rows(s, r, n, store)
+        diffuse_rows(part_hi, part_lo, th, tl, s, r, n, store)
         for k in range(1, peers):
             forward(s, c, k).start()
         cols[s, z, me, r:r + n, :] = ext[s, z, me, r:r + n, :]
@@ -383,6 +385,16 @@
         def _():
             relay(j, True).wait_recv()
             pass_on(j)
+
+    def launch(z):
+        @pl.when(mine == home)
+        def _():
+            for k in range(1, peers):
+                collected(z, k).wait_recv()
+
+            @pl.loop(z * (peers // 2), (z + 1) * (peers // 2))
+            def _(j):
+                pass_on(j)
 
     count = nz * peers // 2
     for c in range(len(parts)):
@@ -398,16 +410,9 @@
             if c == len(parts) - 1:
                 await_relay(s)
 
-        if c == 0:
-            @pl.when(mine == home)
-            def _():
-                for z in range(nz):
-                    for k in range(1, peers):
-                        collected(z, k).wait_recv()
-
-                    @pl.loop(z * (peers // 2), (z + 1) * (peers // 2))
-                    def _(j):
-                        pass_on(j)
+        for z in range(nz):
+            if c == (1, 1)[z]:
+                launch(z)
 
     reach = 24
     part = 64
@@ -507,7 +512,9 @@
             def store(b, total):
                 out_ref[s, z, :, b * BLOCK:(b + 1) * BLOCK] = total
 
-            diffuse_rows(s, 0, rows, store)
+            @pl.when(s < ns - 1 if z == nz - 1 else s < ns)
+            def _():
+                diffuse_rows(part_hi, part_lo, th, tl, s, 0, rows, store)
 
     @pl.loop(0, ns)
     def _(s):
@@ -537,12 +544,25 @@
             relay(j, False).wait_send()
 
 
-def hand_over_kernel(held_ref, out_ref, sem):
+def finish_kernel(held_ref, th, tl, part_hi, part_lo, out_ref, lines, sem, sem_last):
+    ns, nz, rows, nx = held_ref.shape
     copies = [
-        pltpu.make_async_copy(held_ref.at[s], out_ref.at[s], sem.at[s]) for s in range(held_ref.shape[0])
+        pltpu.make_async_copy(held_ref.at[s, z], out_ref.at[s, z], sem.at[s, z])
+        for s in range(ns) for z in range(nz) if s < ns - 1 or z < nz - 1
     ]
     for copy in copies:
         copy.start()
+
+    def store(b, total):
+        lines[b] = total
+        copies.append(
+            pltpu.make_async_copy(
+                lines.at[b], out_ref.at[ns - 1, nz - 1, :, pl.ds(b * BLOCK, BLOCK)], sem_last.at[b]
+            )
+        )
+        copies[-1].start()
+
+    diffuse_rows(part_hi, part_lo, th, tl, ns - 1, 0, rows, store)
     for copy in copies:
         copy.wait()
 
@@ -558,21 +578,23 @@
     dma = pltpu.SemaphoreType.DMA
     result = pl.pallas_call(
         functools.partial(transport_kernel, peers, groups),
-        out_shape=pltpu.VMEM(scalars.shape, f32),
+        out_shape=[
+            pltpu.VMEM(scalars.shape, f32),
+            pltpu.VMEM((2 * ns, BLOCK, nx), bf16),
+            pltpu.VMEM((2 * ns, BLOCK, nx), bf16),
+            pltpu.VMEM((rows, nx), bf16),
+            pltpu.VMEM((rows, nx), bf16),
+        ],
         in_specs=[anywhere, vmem, vmem, vmem, vmem, smem, anywhere],
-        out_specs=vmem,
+        out_specs=[vmem] * 5,
         scratch_shapes=[
             pltpu.VMEM(scalars.shape, f32),
             pltpu.VMEM((nx // 2, nx), f32),
             pltpu.VMEM((2 * ns, nx), f32),
-            pltpu.VMEM((2 * ns, BLOCK, nx), bf16),
-            pltpu.VMEM((2 * ns, BLOCK, nx), bf16),
             pltpu.VMEM((nz, rows, LANES), i32),
             pltpu.VMEM((nz, rows, LANES), i32),
             pltpu.VMEM((nz, 6, rows, nx), f32),
             pltpu.VMEM((nz, 6, ny + 24, width), f32),
-            pltpu.VMEM((rows, nx), bf16),
-            pltpu.VMEM((rows, nx), bf16),
             pltpu.VMEM((ns, nz, peers, rows, width), f32),
             pltpu.VMEM((ns, nz, peers, rows, width), f32),
             pltpu.VMEM((ny, nz * width), bf16),
@@ -596,20 +618,21 @@
             dma((ns, nz, peers - 1)),
         ],
         compiler_params=pltpu.CompilerParams(
-            collective_id=0, has_side_effects=True, vmem_limit_bytes=52 * 2**20
+            collective_id=0, has_side_effects=True, vmem_limit_bytes=42 * 2**20
         ),
     )(
         scalars, velocity_x, velocity_y, shift_x, shift_y[None, :], schmidt,
         jnp.asarray(cosine_table(nx)),
     )
+    result = [pltpu.with_memory_space_constraint(r, pltpu.VMEM) for r in result]
     return pl.pallas_call(
-        hand_over_kernel,
+        finish_kernel,
         out_shape=jax.ShapeDtypeStruct(scalars.shape, f32),
-        in_specs=[anywhere],
+        in_specs=[vmem] * 5,
         out_specs=anywhere,
-        scratch_shapes=[dma((ns,))],
-        compiler_params=pltpu.CompilerParams(vmem_limit_bytes=2**20),
-    )(result)
+        scratch_shapes=[pltpu.VMEM((nx // BLOCK, rows, BLOCK), f32), dma((ns, nz)), dma((nx // BLOCK,))],
+        compiler_params=pltpu.CompilerParams(vmem_limit_bytes=6 * 2**20),
+    )(*result)
 
 
 def transport(peers, groups, scalars, *others):

time: 118 us -> 117 us (level)
    pallas_call x1, Pallas kernels: 116 us -> 115 us  [transport_on_device(): pl.pallas_call(functools.partial(transport_kernel, peers, groups), out_sh...]
where the time goes in v3:
time: 117 us
  Pallas kernels  117 us (100%)
    pallas_call x1, Pallas kernels, transport_on_device(): pl.pallas_call(functools.partial(transport_kernel, peers, groups), out_sh...  115 us

profile of v3, /device:TPU:31, one launch (start us, length us, event | category | flops | bytes accessed | tf_op | source)
XLA Modules:
  0.0 116.6 jit_solution(1931509251922209673)
XLA Ops:
  0.0 114.5 %shard_map.73 = (f32[4,2,128,1024]{3,2,1,0:T(8,128)S(1)}, bf16[8,256,1024]{2,1,0:T(8,128)(2,1)S(1)}, bf16[8,256,1024]{2,1,0:T(8,128)(2,1)S(1)}, bf16[128,1024]{1,0:T(8,128)(2,1)S(1)}, bf16[128,1024]{1,0:T(8,128)(2,1)S(1)}) custom-call(f32[4,2,128,1024]{3,2,1,0:T(8,128)} %q_hbm.1, f32[2,128,256]{2,1,0:T(8,128)} %vx_ref.1, f32[2,128,256]{2,1,0:T(8,128)} %vy_ref.1, ...), custom_call_target="tpu_custom_call" | custom-call | tf_op jit(solution)/shard_map/pallas_call | solution.py:579
  114.5 2.1 %shard_map.74 = f32[4,2,128,1024]{3,2,1,0:T(8,128)} custom-call(f32[4,2,128,1024]{3,2,1,0:T(8,128)S(1)} %get-tuple-element.10.held_ref, bf16[8,256,1024]{2,1,0:T(8,128)(2,1)S(1)} %get-tuple-element.11.th, bf16[8,256,1024]{2,1,0:T(8,128)(2,1)S(1)} %get-tuple-element.12.tl, bf16[128,1024]{1,0:T(8,128)(2,1)S(1)} %get-tuple-element.13.part_hi, ...), custom_call_target="tpu_custom_call" | custom-call | tf_op jit(solution)/shard_map/pallas_call | solution.py:628

commit v4 on v3

--- a/solution.py
+++ b/solution.py
@@ -186,7 +186,7 @@
     q_ref, cos_ref, line, shift_of, place_of, wx, wy,
     ext, cols, col_hi, col_lo, turned, back, held, colv,
     sem_q, sem_c, sendx, recvx, sendv, recvv, send_up, send_down, recv_relay,
-    send1, recv1, send2, recv2,
+    send1, recv1, send2, recv2, send3, recv3,
 ):
     ns, nz, rows, nx = q_ref.shape
     ny = rows * peers
@@ -357,11 +357,22 @@
             device_id={"space": dest}, device_id_type=MESH,
         )
 
-    def backward(s, z, k):
+    def backward(s, k):
         dest = lax.rem(me + k, peers)
         return pltpu.make_async_remote_copy(
-            src_ref=turned.at[s, dest, z], dst_ref=back.at[s, me, z],
-            send_sem=send2.at[s, z, k - 1], recv_sem=recv2.at[s, z, k - 1],
+            src_ref=turned.at[s, dest], dst_ref=back.at[s, me],
+            send_sem=send2.at[s, k - 1], recv_sem=recv2.at[s, k - 1],
+            device_id={"space": dest}, device_id_type=MESH,
+        )
+
+    pieces = ((0, 0, rows), (1, 0, half), (1, half, half))
+
+    def backward_last(c, k):
+        z, r, n = pieces[c]
+        dest = lax.rem(me + k, peers)
+        return pltpu.make_async_remote_copy(
+            src_ref=turned.at[ns - 1, dest, z, pl.ds(r, n), :], dst_ref=back.at[ns - 1, me, z, pl.ds(r, n), :],
+            send_sem=send3.at[c, k - 1], recv_sem=recv3.at[c, k - 1],
             device_id={"space": dest}, device_id_type=MESH,
         )
 
@@ -494,35 +505,57 @@
                     turned[s, a * (BLOCK // rows) + h, z] = total[
                         h * rows:(h + 1) * rows, z * width:(z + 1) * width
                     ]
+        @pl.when(s < ns - 1)
+        def _():
+            for k in range(1, peers):
+                backward(s, k).start()
+
+        @pl.when(s == ns - 1)
+        def _():
+            for c in range(len(pieces)):
+                for k in range(1, peers):
+                    backward_last(c, k).start()
+
+        back[s, me] = turned[s, me]
+
+    def returned(s, z):
+        return lambda at: jnp.concatenate([back[s, p, z, at, :] for p in range(peers)], axis=1)
+
+    def finish(s, z):
+        def store(b, total):
+            out_ref[s, z, :, b * BLOCK:(b + 1) * BLOCK] = total
+
+        diffuse_rows(part_hi, part_lo, th, tl, s, 0, rows, store)
+
+    @pl.loop(0, ns - 1)
+    def _(s):
+        for k in range(1, peers):
+            backward(s, k).wait_recv()
         for z in range(nz):
-            for k in range(1, peers):
-                backward(s, z, k).start()
-        back[s, me] = turned[s, me]
-
-    @pl.loop(0, ns)
-    def _(s):
-        for z in range(nz):
-            for k in range(1, peers):
-                backward(s, z, k).wait_recv()
-            remesh_rows(
-                z, 0, rows,
-                lambda at: jnp.concatenate([back[s, p, z, at, :] for p in range(peers)], axis=1),
-            )
-
-            def store(b, total):
-                out_ref[s, z, :, b * BLOCK:(b + 1) * BLOCK] = total
-
-            @pl.when(s < ns - 1 if z == nz - 1 else s < ns)
-            def _():
-                diffuse_rows(part_hi, part_lo, th, tl, s, 0, rows, store)
+            remesh_rows(z, 0, rows, returned(s, z))
+            finish(s, z)
+
+    for c, (z, r, n) in enumerate(pieces):
+        for k in range(1, peers):
+            backward_last(c, k).wait_recv()
+        remesh_rows(z, r, n, returned(ns - 1, z))
+        if c == 0:
+            finish(ns - 1, z)
 
     @pl.loop(0, ns)
     def _(s):
         for k in range(1, peers):
             for c in range(len(parts)):
                 forward(s, c, k).wait_send()
-            for z in range(nz):
-                backward(s, z, k).wait_send()
+
+    @pl.loop(0, ns - 1)
+    def _(s):
+        for k in range(1, peers):
+            backward(s, k).wait_send()
+
+    for c in range(len(pieces)):
+        for k in range(1, peers):
+            backward_last(c, k).wait_send()
 
     for c in range(len(parts)):
         for k in range(1, groups):
@@ -614,8 +647,10 @@
             dma((count,)),
             dma((ns, 3, peers - 1)),
             dma((ns, 3, peers - 1)),
-            dma((ns, nz, peers - 1)),
-            dma((ns, nz, peers - 1)),
+            dma((ns - 1, peers - 1)),
+            dma((ns - 1, peers - 1)),
+            dma((3, peers - 1)),
+            dma((3, peers - 1)),
         ],
         compiler_params=pltpu.CompilerParams(
             collective_id=0, has_side_effects=True, vmem_limit_bytes=42 * 2**20

time: 117 us -> 116 us (level)
  Pallas kernels: 117 us -> 115 us
where the time goes in v4:
time: 116 us; the launch traced here: 115 us
  Pallas kernels  115 us (99%)
    pallas_call x1, Pallas kernels, transport_on_device(): pl.pallas_call(functools.partial(transport_kernel, peers, groups), out_sh...  113 us

profile of v4, /device:TPU:31, one launch (start us, length us, event | category | flops | bytes accessed | tf_op | source)
XLA Modules:
  0.0 115.5 jit_solution(9841073272378446605)
XLA Ops:
  0.0 113.4 %shard_map.73 = (f32[4,2,128,1024]{3,2,1,0:T(8,128)S(1)}, bf16[8,256,1024]{2,1,0:T(8,128)(2,1)S(1)}, bf16[8,256,1024]{2,1,0:T(8,128)(2,1)S(1)}, bf16[128,1024]{1,0:T(8,128)(2,1)S(1)}, bf16[128,1024]{1,0:T(8,128)(2,1)S(1)}) custom-call(f32[4,2,128,1024]{3,2,1,0:T(8,128)} %q_hbm.1, f32[2,128,256]{2,1,0:T(8,128)} %vx_ref.1, f32[2,128,256]{2,1,0:T(8,128)} %vy_ref.1, ...), custom_call_target="tpu_custom_call" | custom-call | tf_op jit(solution)/shard_map/pallas_call | solution.py:612
  113.4 2.1 %shard_map.74 = f32[4,2,128,1024]{3,2,1,0:T(8,128)} custom-call(f32[4,2,128,1024]{3,2,1,0:T(8,128)S(1)} %get-tuple-element.10.held_ref, bf16[8,256,1024]{2,1,0:T(8,128)(2,1)S(1)} %get-tuple-element.11.th, bf16[8,256,1024]{2,1,0:T(8,128)(2,1)S(1)} %get-tuple-element.12.tl, bf16[128,1024]{1,0:T(8,128)(2,1)S(1)} %get-tuple-element.13.part_hi, ...), custom_call_target="tpu_custom_call" | custom-call | tf_op jit(solution)/shard_map/pallas_call | solution.py:663

commit v5 on v4

--- a/solution.py
+++ b/solution.py
@@ -260,7 +260,7 @@
         def _():
             relay(j, False).start()
 
-    for k in range(1, groups):
+    for k in reversed(range(1, groups)):
         spread(0, k).start()
     for z in range(nz):
         for h in range(ratio):

time: 116 us -> 116 us (level)
  no operation moved by 1% of the time
where the time goes in v5:
time: 116 us
  Pallas kernels  116 us (100%)
    pallas_call x1, Pallas kernels, transport_on_device(): pl.pallas_call(functools.partial(transport_kernel, peers, groups), out_sh...  113 us

profile of v5, /device:TPU:31, one launch (start us, length us, event | category | flops | bytes accessed | tf_op | source)
XLA Modules:
  0.0 115.6 jit_solution(10941208490976652060)
XLA Ops:
  0.0 113.5 %shard_map.73 = (f32[4,2,128,1024]{3,2,1,0:T(8,128)S(1)}, bf16[8,256,1024]{2,1,0:T(8,128)(2,1)S(1)}, bf16[8,256,1024]{2,1,0:T(8,128)(2,1)S(1)}, bf16[128,1024]{1,0:T(8,128)(2,1)S(1)}, bf16[128,1024]{1,0:T(8,128)(2,1)S(1)}) custom-call(f32[4,2,128,1024]{3,2,1,0:T(8,128)} %q_hbm.1, f32[2,128,256]{2,1,0:T(8,128)} %vx_ref.1, f32[2,128,256]{2,1,0:T(8,128)} %vy_ref.1, ...), custom_call_target="tpu_custom_call" | custom-call | tf_op jit(solution)/shard_map/pallas_call | solution.py:612
  113.5 2.1 %shard_map.74 = f32[4,2,128,1024]{3,2,1,0:T(8,128)} custom-call(f32[4,2,128,1024]{3,2,1,0:T(8,128)S(1)} %get-tuple-element.10.held_ref, bf16[8,256,1024]{2,1,0:T(8,128)(2,1)S(1)} %get-tuple-element.11.th, bf16[8,256,1024]{2,1,0:T(8,128)(2,1)S(1)} %get-tuple-element.12.tl, bf16[128,1024]{1,0:T(8,128)(2,1)S(1)} %get-tuple-element.13.part_hi, ...), custom_call_target="tpu_custom_call" | custom-call | tf_op jit(solution)/shard_map/pallas_call | solution.py:663
